TPU v7x, 32 devices: a whole 2x2x4 slice. The times are simulated.
32 devices in a mesh: slab: 8 (over z, y), grp: 4 (over x, core).
Axes of the slice: x: 2, y: 2, z: 4, core: 2. Of those that a mesh axis runs over, the one named last changes fastest.
Arguments:
- positions: float32 [32, 16, 3, 128], P('slab', 'grp'), may hold values from 0 to 1
- sketch: bfloat16 [32, 16, 128, 256], P('slab', 'grp'), may hold values from -6 to 6
- counts: int32 [32, 16], P('slab', 'grp'), may hold values from 32 to 128, as said below
- neighbours: int32 [32, 16, 8], P('slab', 'grp'), may hold values from 0 to 8, as said below
Outputs:
- basis: bfloat16 [32, 16, 128, 256], P('slab', 'grp')
- factor: float32 [256, 256], replicated
Inputs may be any that keep to these rules, and one draw needn't show every extreme that they name: `counts`: the first block of every device's region of 4 x 4 blocks is full. `neighbours`: a code is 3 (dz + 1) + (dy + 1) for offsets dz, dy in -1, 0, 1; the codes of one block are distinct and always include 4 (the block itself); each block leaves out exactly one of its nine codes, and the lists are symmetric: block a lists block b if and only if block b lists block a; the left-out pairs lie inside aligned 2 x 2 squares of blocks.
All inputs are finite; a program needn't handle non-finite values.
Results may differ from a plain program's by a relative error of at most 0.017.
Values may be sent and summed in bfloat16 or wider, within the bound.
A program may use at most 64 MiB of HBM per device.

v0:
```python
import math
import jax
import jax.numpy as jnp
from jax import lax
from jax.sharding import PartitionSpec as P


def padded(shard, sides, width):
    for axis, dim in sides:
        count, length = (lax.axis_size(axis), shard.shape[dim])
        up = [(i, (i + 1) % count) for i in range(count)]
        down = [(j, i) for i, j in up]
        last = lax.slice_in_dim(shard, length - width, length, axis=dim)
        leading = lax.slice_in_dim(shard, 0, width, axis=dim)
        before = lax.ppermute(last, axis, up)
        after = lax.ppermute(leading, axis, down)
        shard = jnp.concatenate([before, shard, after], axis=dim)
    return shard


def kernel_tile(own_pos, other_pos, shift_z, shift_y):
    diff_z = other_pos[..., 0, None, :] + shift_z[..., None, None] - own_pos[..., 0, :, None]
    diff_y = other_pos[..., 1, None, :] + shift_y[..., None, None] - own_pos[..., 1, :, None]
    diff_x = other_pos[..., 2, None, :] - own_pos[..., 2, :, None]
    radius = jnp.sqrt(diff_z * diff_z + diff_y * diff_y + diff_x * diff_x)
    taper = jnp.maximum(1.0 - radius, 0.0)
    return taper**4 * (4.0 * radius + 1.0)


def on_device(positions, sketch, counts, neighbours):
    blocks_z, blocks_y, _, points = positions.shape
    columns = sketch.shape[3]
    live_mask = (
        lax.broadcasted_iota(jnp.int32, (blocks_z, blocks_y, points), 2) < counts[:, :, None]
    )
    masked = jnp.where(live_mask[..., None], sketch, jnp.zeros_like(sketch))
    wide_pos, wide_rows = (
        padded(positions.astype(jnp.bfloat16), (("slab", 0), ("grp", 1)), 1).astype(
            positions.dtype
        ),
        padded(masked, (("slab", 0), ("grp", 1)), 1),
    )
    pos_table = wide_pos.reshape(-1, 3, points)
    row_table = wide_rows.reshape(-1, points, columns)
    own_pos = positions.reshape(-1, 3, points)
    row_ids = lax.broadcasted_iota(jnp.int32, (blocks_z, blocks_y), 0)
    col_ids = lax.broadcasted_iota(jnp.int32, (blocks_z, blocks_y), 1)
    image = jnp.zeros((blocks_z * blocks_y, points, columns), jnp.float32)
    for slot_index in range(neighbours.shape[2]):
        offset_code = neighbours[:, :, slot_index]
        shift_z = offset_code // 3 - 1
        shift_y = offset_code % 3 - 1
        source_ids = ((row_ids + 1 + shift_z) * (blocks_y + 2) + col_ids + 1 + shift_y).reshape(-1)
        other_pos = jnp.take(pos_table, source_ids, axis=0)
        other_rows = jnp.take(row_table, source_ids, axis=0)
        weights = kernel_tile(
            own_pos,
            other_pos,
            shift_z.reshape(-1).astype(jnp.float32),
            shift_y.reshape(-1).astype(jnp.float32),
        ).astype(jnp.bfloat16)
        image = image + jnp.einsum(
            "bij,bjr->bir", weights, other_rows, preferred_element_type=jnp.float32
        )
    image = jnp.where(live_mask.reshape(-1, points)[..., None], image, jnp.zeros_like(image))
    flat_rows = image.reshape(-1, columns)
    gram_local = jnp.dot(
        flat_rows.T, flat_rows, preferred_element_type=jnp.float32, precision=lax.Precision.HIGHEST
    )
    gram_total = lax.psum(gram_local, ("slab", "grp"))
    lower_factor = jnp.linalg.cholesky(gram_total)
    solved = lax.linalg.triangular_solve(lower_factor, flat_rows.T, left_side=True, lower=True)
    total_rows = lax.axis_size("slab") * blocks_z * lax.axis_size("grp") * blocks_y * points
    scale_rows = math.sqrt(total_rows)
    basis = (
        (solved.T * scale_rows).reshape(blocks_z, blocks_y, points, columns).astype(jnp.bfloat16)
    )
    factor = lower_factor.T / scale_rows
    return (basis, factor)


def solution(mesh):
    placed = (
        P("slab", "grp", None, None),
        P("slab", "grp", None, None),
        P("slab", "grp"),
        P("slab", "grp", None),
    )
    return jax.shard_map(
        on_device,
        mesh=mesh,
        in_specs=placed,
        out_specs=(P("slab", "grp", None, None), P()),
        check_vma=False,
    )
```

profile of v0, /device:TPU:0, one launch (start us, length us, event | category | flops | bytes accessed | tf_op | source)
XLA Modules:
  0.0 279.9 jit_solution(16708323109046703102)
XLA Ops:
  7.2 0.7 convert_element_type.155
  8.0 3.0 %collective-permute-start = (bf16[1,4,3,128]{3,1,2,0:T(4,128)(2,1)S(1)}, bf16[1,4,3,128]{3,1,2,0:T(4,128)(2,1)S(1)}, u32[]{:S(2)}, u32[]{:S(2)}) collective-permute-start(bf16[1,4,3,128]{3,1,2,0:T(4,128)(2,1)S(1)} %get-tuple-element.121), channel_id=1, source_target_pairs={{0,4},{4,8},{8,12},{12,16},{16,20},{20,24},{24,28},{28,0},{1,5},{5... | collective-permute-start | bytes 9224 | tf_op jit(solution)/shard_map/ppermute | solution.py:15
  11.0 3.1 %collective-permute-start.1 = (bf16[1,4,3,128]{3,1,2,0:T(4,128)(2,1)S(1)}, bf16[1,4,3,128]{3,1,2,0:T(4,128)(2,1)S(1)}, u32[]{:S(2)}, u32[]{:S(2)}) collective-permute-start(bf16[1,4,3,128]{3,1,2,0:T(4,128)(2,1)S(1)} %get-tuple-element.122), channel_id=1, source_target_pairs={{4,0},{8,4},{12,8},{16,12},{20,16},{24,20},{28,24},{0,28},{5,1},{9... | collective-permute-start | bytes 9224 | tf_op jit(solution)/shard_map/ppermute | solution.py:16
  14.1 0.8 iota_compare_fusion.3
  14.9 1.5 broadcast_select_fusion
  16.5 4.7 %collective-permute-start.5 = (bf16[1,4,128,256]{3,2,1,0:T(8,128)(2,1)S(1)}, bf16[1,4,128,256]{3,2,1,0:T(8,128)(2,1)S(1)}, u32[]{:S(2)}, u32[]{:S(2)}) collective-permute-start(bf16[1,4,128,256]{3,2,1,0:T(8,128)(2,1)S(1)} %get-tuple-element.85), channel_id=1, source_target_pairs={{4,0},{8,4},{12,8},{16,12},{20,16},{24,20},{28,24},{0,28},{5,1},{9... | collective-permute-start | bytes 786440 | tf_op jit(solution)/shard_map/ppermute | solution.py:16
  21.3 0.7 fusion.121
  22.0 1.3 remainder_reduce_fusion
  26.2 1.7 collective-permute-start.3
  28.0 1.3 collective-permute-done.2
  34.4 0.7 slice_add_fusion.11
  36.6 1.7 collective-permute-start.6
  39.2 0.7 slice_add_fusion.15
  39.9 6.3 %collective-permute-done.6 = bf16[6,1,128,256]{3,2,1,0:T(8,128)(2,1)S(1)} collective-permute-done((bf16[6,1,128,256]{3,2,1,0:T(8,128)(2,1)S(1)}, bf16[6,1,128,256]{3,2,1,0:T(8,128)(2,1)S(1)}, u32[]{:S(2)}, u32[]{:S(2)}) %collective-permute-start.6) | collective-permute-done | bytes 393248 | tf_op jit(solution)/shard_map/ppermute | solution.py:15
  46.2 1.0 collective-permute-done.7
  47.2 1.4 pad_maximum_fusion
  49.2 1.7 gather_fusion.13
  50.9 1.7 gather_fusion.11
  52.6 1.7 gather_fusion.9
  54.3 1.7 gather_fusion.7
  56.0 1.7 gather_fusion.5
  57.8 1.8 gather_fusion.3
  59.6 1.8 gather_fusion.1
  61.4 2.4 fusion.5
  63.9 1.7 fusion.7
  65.6 1.7 fusion.9
  67.4 1.7 fusion.11
  69.2 1.7 fusion.13
  71.0 1.7 fusion.17
  72.7 1.7 fusion.15
  74.5 2.8 add_select_fusion
  77.2 4.2 %convolution_bitcast_fusion = f32[256,256]{0,1:T(8,128)} fusion(f32[16,128,256]{2,1,0:T(8,128)S(1)} %add_select_fusion), kind=kOutput, calls=%fused_computation.23 | convolution fusion | flops 1610612736 | bytes 2359296 | tf_op jit(solution)/shard_map/dot_general | solution.py:67
  81.4 122.8 %all-reduce.3.cloned.1.call-done = f32[256,256]{0,1:T(8,128)} async-done(((f32[256,256]{0,1:T(8,128)}), f32[256,256]{0,1:T(8,128)}) %all-reduce.3.cloned.1.call-update) | async-done | bytes 262160 | tf_op jit(solution)/shard_map/psum | solution.py:70
  204.2 1.1 copy.23
  205.3 1.0 fusion.107
  206.3 11.7 %cholesky.50 = f32[128,128]{1,0:T(8,128)S(1)} custom-call(f32[128,128]{1,0:T(8,128)S(1)} %cholesky.118), custom_call_target="Cholesky" | custom-call | tf_op jit(solution)/shard_map/jit(cholesky)/cholesky | solution.py:71
  218.7 9.8 %custom-call.14 = f32[1,128,128]{1,2,0:T(8,128)S(1)} custom-call(f32[1,128,128]{2,1,0:T(8,128)S(1)} %get-tuple-element.91), custom_call_target="InvertDiagBlocksLowerTriangular" | custom-call | tf_op jit(solution)/shard_map/jit(cholesky)/cholesky | solution.py:71
  229.0 11.9 %cholesky.105 = f32[128,128]{1,0:T(8,128)S(1)} custom-call(f32[128,128]{1,0:T(8,128)S(1)} %convolution_subtract_fusion.1), custom_call_target="Cholesky" | custom-call | tf_op jit(solution)/shard_map/jit(cholesky)/cholesky | solution.py:71
  241.0 0.7 compare_reduce_fusion
  243.0 0.8 copy.25
  243.9 4.0 %while.1 = (s32[]{:T(128)}, f32[256,256]{1,0:T(8,128)S(1)}, s32[2,2]{1,0:T(2,128)S(1)}, f32[2,128,128]{2,1,0:T(8,128)S(1)}, s32[]{:T(128)}) while((s32[]{:T(128)}, f32[256,256]{1,0:T(8,128)S(1)}, s32[2,2]{1,0:T(2,128)S(1)}, f32[2,128,128]{2,1,0:T(8,128)S(1)}, s32[]{:T(128)}) %tuple.117), condition=%wide.while_cond, body=%wide.while_body.sunk | while | flops 2 | bytes 131189 | solution.py:72
  244.6 1.3 bitcast_dynamic-update-slice_fusion.2
  246.6 1.3 bitcast_dynamic-update-slice_fusion.2
  247.9 19.7 %custom-call.15 = f32[2,128,128]{1,2,0:T(8,128)S(1)} custom-call(f32[2,128,128]{2,1,0:T(8,128)S(1)} %get-tuple-element.11), custom_call_target="InvertDiagBlocksLowerTriangular" | custom-call | tf_op jit(solution)/shard_map/triangular_solve | solution.py:72
  267.6 1.1 fusion.2
  268.7 1.8 convolution_subtract_fusion
  270.5 1.1 fusion.110
  271.8 1.3 copy.29
  (190 shorter events, 13.7 us)
Async XLA Ops:
  7.2 14.1 %copy-start.9 = (f32[4,4,3,128]{3,1,2,0:T(4,128)S(1)}, f32[4,4,3,128]{3,1,2,0:T(4,128)}, u32[]{:S(2)}) copy-start(f32[4,4,3,128]{3,1,2,0:T(4,128)} %param.8) | copy-start | bytes 73732
  7.2 14.0 %copy-start.20 = (s32[4,4]{1,0:T(4,128)S(1)}, s32[4,4]{1,0:T(4,128)}, u32[]{:S(2)}) copy-start(s32[4,4]{1,0:T(4,128)} %param.10) | copy-start | bytes 196
  7.2 14.1 %copy-start = (s32[4,4,8]{2,1,0:T(4,128)S(1)}, s32[4,4,8]{2,1,0:T(4,128)}, u32[]{:S(2)}) copy-start(s32[4,4,8]{2,1,0:T(4,128)} %param.11) | copy-start | bytes 1540
  7.2 197.0 %all-reduce.3.cloned.1.call-start = ((), (), s32[]{:S(2)}) async-start(), calls=%async_computation | async-start | bytes 524288 | tf_op jit(solution)/shard_map/psum | solution.py:70
  8.0 18.1 %collective-permute-start = (bf16[1,4,3,128]{3,1,2,0:T(4,128)(2,1)S(1)}, bf16[1,4,3,128]{3,1,2,0:T(4,128)(2,1)S(1)}, u32[]{:S(2)}, u32[]{:S(2)}) collective-permute-start(bf16[1,4,3,128]{3,1,2,0:T(4,128)(2,1)S(1)} %get-tuple-element.121), channel_id=1, source_target_pairs={{0,4},{4,8},{8,12},{12,16},{16,20},{20,24},{24,28},{28,0},{1,5},{5... | collective-permute-start | bytes 9224 | tf_op jit(solution)/shard_map/ppermute | solution.py:15
  11.0 15.1 %collective-permute-start.1 = (bf16[1,4,3,128]{3,1,2,0:T(4,128)(2,1)S(1)}, bf16[1,4,3,128]{3,1,2,0:T(4,128)(2,1)S(1)}, u32[]{:S(2)}, u32[]{:S(2)}) collective-permute-start(bf16[1,4,3,128]{3,1,2,0:T(4,128)(2,1)S(1)} %get-tuple-element.122), channel_id=1, source_target_pairs={{4,0},{8,4},{12,8},{16,12},{20,16},{24,20},{28,24},{0,28},{5,1},{9... | collective-permute-start | bytes 9224 | tf_op jit(solution)/shard_map/ppermute | solution.py:16
  16.4 20.1 %collective-permute-start.4 = (bf16[1,4,128,256]{3,2,1,0:T(8,128)(2,1)S(1)}, bf16[1,4,128,256]{3,2,1,0:T(8,128)(2,1)S(1)}, u32[]{:S(2)}, u32[]{:S(2)}) collective-permute-start(bf16[1,4,128,256]{3,2,1,0:T(8,128)(2,1)S(1)} %get-tuple-element.84), channel_id=1, source_target_pairs={{0,4},{4,8},{8,12},{12,16},{16,20},{20,24},{24,28},{28,0},{1,5},{5... | collective-permute-start | bytes 786440 | tf_op jit(solution)/shard_map/ppermute | solution.py:15
  16.5 20.0 %collective-permute-start.5 = (bf16[1,4,128,256]{3,2,1,0:T(8,128)(2,1)S(1)}, bf16[1,4,128,256]{3,2,1,0:T(8,128)(2,1)S(1)}, u32[]{:S(2)}, u32[]{:S(2)}) collective-permute-start(bf16[1,4,128,256]{3,2,1,0:T(8,128)(2,1)S(1)} %get-tuple-element.85), channel_id=1, source_target_pairs={{4,0},{8,4},{12,8},{16,12},{20,16},{24,20},{28,24},{0,28},{5,1},{9... | collective-permute-start | bytes 786440 | tf_op jit(solution)/shard_map/ppermute | solution.py:16
  25.8 7.3 %copy-start.28 = (pred[16]{0:T(512)(128)(4,1)}, pred[16]{0:T(512)(128)(4,1)S(1)}, u32[]{:S(2)}) copy-start(pred[16]{0:T(512)(128)(4,1)S(1)} %get-tuple-element.50) | copy-start | bytes 52
  25.9 7.9 %copy-start.34 = (pred[16]{0:T(512)(128)(4,1)}, pred[16]{0:T(512)(128)(4,1)S(1)}, u32[]{:S(2)}) copy-start(pred[16]{0:T(512)(128)(4,1)S(1)} %get-tuple-element.131) | copy-start | bytes 52
  25.9 7.9 %copy-start.36 = (pred[16]{0:T(512)(128)(4,1)}, pred[16]{0:T(512)(128)(4,1)S(1)}, u32[]{:S(2)}) copy-start(pred[16]{0:T(512)(128)(4,1)S(1)} %get-tuple-element.129) | copy-start | bytes 52
  25.9 7.9 %copy-start.38 = (pred[16]{0:T(512)(128)(4,1)}, pred[16]{0:T(512)(128)(4,1)S(1)}, u32[]{:S(2)}) copy-start(pred[16]{0:T(512)(128)(4,1)S(1)} %get-tuple-element.127) | copy-start | bytes 52
  25.9 7.9 %copy-start.40 = (pred[16]{0:T(512)(128)(4,1)}, pred[16]{0:T(512)(128)(4,1)S(1)}, u32[]{:S(2)}) copy-start(pred[16]{0:T(512)(128)(4,1)S(1)} %get-tuple-element.125) | copy-start | bytes 52
  25.9 10.4 %copy-start.42 = (pred[16]{0:T(512)(128)(4,1)}, pred[16]{0:T(512)(128)(4,1)S(1)}, u32[]{:S(2)}) copy-start(pred[16]{0:T(512)(128)(4,1)S(1)} %get-tuple-element.123) | copy-start | bytes 52
  25.9 13.3 %copy-start.30 = (pred[16]{0:T(512)(128)(4,1)}, pred[16]{0:T(512)(128)(4,1)S(1)}, u32[]{:S(2)}) copy-start(pred[16]{0:T(512)(128)(4,1)S(1)} %get-tuple-element.133) | copy-start | bytes 52
  25.9 13.3 %copy-start.32 = (pred[16]{0:T(512)(128)(4,1)}, pred[16]{0:T(512)(128)(4,1)S(1)}, u32[]{:S(2)}) copy-start(pred[16]{0:T(512)(128)(4,1)S(1)} %get-tuple-element.135) | copy-start | bytes 52
  25.9 7.1 %copy-start.21 = (s32[1024]{0:T(1024)}, s32[1024]{0:T(1024)S(1)}, u32[]{:S(2)}) copy-start(s32[1024]{0:T(1024)S(1)} %pad_clamp_fusion.1) | copy-start | bytes 12292
  26.0 7.1 %copy-start.22 = (s32[1024]{0:T(1024)}, s32[1024]{0:T(1024)S(1)}, u32[]{:S(2)}) copy-start(s32[1024]{0:T(1024)S(1)} %pad_clamp_fusion.2) | copy-start | bytes 12292
  26.0 7.2 %copy-start.23 = (s32[1024]{0:T(1024)}, s32[1024]{0:T(1024)S(1)}, u32[]{:S(2)}) copy-start(s32[1024]{0:T(1024)S(1)} %pad_clamp_fusion.3) | copy-start | bytes 12292
  26.0 7.1 %copy-start.24 = (s32[1024]{0:T(1024)}, s32[1024]{0:T(1024)S(1)}, u32[]{:S(2)}) copy-start(s32[1024]{0:T(1024)S(1)} %pad_clamp_fusion.4) | copy-start | bytes 12292
  26.0 7.1 %copy-start.25 = (s32[1024]{0:T(1024)}, s32[1024]{0:T(1024)S(1)}, u32[]{:S(2)}) copy-start(s32[1024]{0:T(1024)S(1)} %pad_clamp_fusion.5) | copy-start | bytes 12292
  26.1 10.3 %copy-start.26 = (s32[1024]{0:T(1024)}, s32[1024]{0:T(1024)S(1)}, u32[]{:S(2)}) copy-start(s32[1024]{0:T(1024)S(1)} %pad_clamp_fusion.6) | copy-start | bytes 12292
  26.2 3.1 %collective-permute-start.2 = (bf16[6,1,3,128]{3,1,2,0:T(2,128)(2,1)S(1)}, bf16[6,1,3,128]{3,1,2,0:T(2,128)(2,1)S(1)}, u32[]{:S(2)}, u32[]{:S(2)}) collective-permute-start(bf16[6,1,3,128]{3,1,2,0:T(2,128)(2,1)S(1)} %get-tuple-element.119), channel_id=1, source_target_pairs={{0,1},{1,2},{2,3},{3,0},{4,5},{5,6},{6,7},{7,4},{8,9},{9,10},{10,1... | collective-permute-start | bytes 13832 | tf_op jit(solution)/shard_map/ppermute | solution.py:15
  26.2 3.1 %collective-permute-start.3 = (bf16[6,1,3,128]{3,1,2,0:T(2,128)(2,1)S(1)}, bf16[6,1,3,128]{3,1,2,0:T(2,128)(2,1)S(1)}, u32[]{:S(2)}, u32[]{:S(2)}) collective-permute-start(bf16[6,1,3,128]{3,1,2,0:T(2,128)(2,1)S(1)} %get-tuple-element.120), channel_id=1, source_target_pairs={{1,0},{2,1},{3,2},{0,3},{5,4},{6,5},{7,6},{4,7},{9,8},{10,9},{11,1... | collective-permute-start | bytes 13832 | tf_op jit(solution)/shard_map/ppermute | solution.py:16
  28.0 8.4 %copy-start.27 = (s32[1024]{0:T(1024)}, s32[1024]{0:T(1024)S(1)}, u32[]{:S(2)}) copy-start(s32[1024]{0:T(1024)S(1)} %pad_clamp_fusion.7) | copy-start | bytes 12292
  36.5 9.7 %copy-start.1 = (bf16[1,4,128,256]{3,2,1,0:T(8,128)(2,1)}, bf16[1,4,128,256]{3,2,1,0:T(8,128)(2,1)S(1)}, u32[]{:S(2)}) copy-start(bf16[1,4,128,256]{3,2,1,0:T(8,128)(2,1)S(1)} %collective-permute-done.4) | copy-start | bytes 786436
  36.5 9.7 %copy-start.2 = (bf16[1,4,128,256]{3,2,1,0:T(8,128)(2,1)}, bf16[1,4,128,256]{3,2,1,0:T(8,128)(2,1)S(1)}, u32[]{:S(2)}) copy-start(bf16[1,4,128,256]{3,2,1,0:T(8,128)(2,1)S(1)} %collective-permute-done.5) | copy-start | bytes 786436
  36.6 9.6 %collective-permute-start.6 = (bf16[6,1,128,256]{3,2,1,0:T(8,128)(2,1)S(1)}, bf16[6,1,128,256]{3,2,1,0:T(8,128)(2,1)S(1)}, u32[]{:S(2)}, u32[]{:S(2)}) collective-permute-start(bf16[6,1,128,256]{3,2,1,0:T(8,128)(2,1)S(1)} %get-tuple-element.82), channel_id=1, source_target_pairs={{0,1},{1,2},{2,3},{3,0},{4,5},{5,6},{6,7},{7,4},{8,9},{9,10},{10,1... | collective-permute-start | bytes 1179656 | tf_op jit(solution)/shard_map/ppermute | solution.py:15
  38.3 8.9 %collective-permute-start.7 = (bf16[6,1,128,256]{3,2,1,0:T(8,128)(2,1)S(1)}, bf16[6,1,128,256]{3,2,1,0:T(8,128)(2,1)S(1)}, u32[]{:S(2)}, u32[]{:S(2)}) collective-permute-start(bf16[6,1,128,256]{3,2,1,0:T(8,128)(2,1)S(1)} %get-tuple-element.83), channel_id=1, source_target_pairs={{1,0},{2,1},{3,2},{0,3},{5,4},{6,5},{7,6},{4,7},{9,8},{10,9},{11,1... | collective-permute-start | bytes 1179656 | tf_op jit(solution)/shard_map/ppermute | solution.py:16
  57.8 3.6 %copy-start.43 = (pred[16]{0:T(512)(128)(4,1)S(1)}, pred[16]{0:T(512)(128)(4,1)}, u32[]{:S(2)}) copy-start(pred[16]{0:T(512)(128)(4,1)} %copy-done.42) | copy-start | bytes 52
  61.4 2.4 copy-start.8
  61.4 2.4 copy-start.41
  65.6 1.7 copy-start.6
  67.3 1.8 copy-start.5
  67.3 1.8 copy-start.11
  67.4 1.8 copy-start.12
  67.4 1.8 copy-start.13
  67.4 1.8 copy-start.35
  69.1 1.8 copy-start.4
  69.1 1.8 copy-start.17
  69.2 1.8 copy-start.18
  69.2 1.8 copy-start.19
  69.2 1.8 copy-start.33
  70.9 1.8 copy-start.3
  70.9 1.8 copy-start.14
  71.0 1.8 copy-start.15
  71.0 1.8 copy-start.16
  71.0 1.8 copy-start.31
  (5 other events, 8.6 us)
Sparse Core Ops, SparseCore 0:
  81.5 122.6 all-reduce.2
where the time goes:
time: 280 us
  waiting for transfers between devices  131 us (47%)
  other arithmetic  66.1 us (24%)
  local copies, waits for them, and re-layouts  27.4 us (10%)
  matrix products  24 us (9%)
  between operations  16.4 us (6%)
  starting transfers between devices  14.6 us (5%)
    psum x1, waiting for transfers between devices, on_device(): gram_total = lax.psum(gram_local, ('slab', 'grp'))  123 us
    another operation x7, other arithmetic, on_device(): lower_factor = jnp.linalg.cholesky(gram_total)  34.8 us
    another operation x2, other arithmetic, on_device(): lax.linalg.triangular_solve(lower_factor, flat_rows.T, left_side=True, lo...  19.7 us
    dot_general x8, matrix products, on_device(): jnp.einsum('bij,bjr->bir', weights, other_rows, preferred_element_type=jn...  15.4 us
    gather x8, local copies, waits for them, and re-layouts, on_device(): other_rows = jnp.take(row_table, source_ids, axis=0)  12.8 us
    ppermute x4, starting transfers between devices, padded(): after = lax.ppermute(leading, axis, down)  9.73 us
    ppermute x4, waiting for transfers between devices, padded(): before = lax.ppermute(last, axis, up)  7.6 us
  transfers between devices with their start and end apart: 9, of which 4 were waited for; matrix products, arithmetic and copies ran while one was open for 5% of the time, Pallas kernels for 0%

commit v1 on v0

--- a/solution.py
+++ b/solution.py
@@ -67,7 +67,7 @@
     gram_local = jnp.dot(
         flat_rows.T, flat_rows, preferred_element_type=jnp.float32, precision=lax.Precision.HIGHEST
     )
-    gram_total = lax.psum(gram_local, ("slab", "grp"))
+    gram_total = lax.psum(lax.psum(gram_local, "grp"), "slab")
     lower_factor = jnp.linalg.cholesky(gram_total)
     solved = lax.linalg.triangular_solve(lower_factor, flat_rows.T, left_side=True, lower=True)
     total_rows = lax.axis_size("slab") * blocks_z * lax.axis_size("grp") * blocks_y * points

time: 280 us -> 261 us (0.932)
  waiting for transfers between devices: 131 us -> 112 us
    psum x1 -> x2, waiting for transfers between devices: 123 us -> 104 us  [on_device(): gram_total = lax.psum(lax.psum(gram_local, 'grp'), 'slab')]
  transfers between devices with their start and end apart: 9 -> 10, of which waited for: 4 -> 5; matrix products, arithmetic and copies ran while one was open for 5% -> 6% of each run, Pallas kernels for 0% -> 0%
where the time goes in v1:
time: 261 us
  waiting for transfers between devices  112 us (43%)
  other arithmetic  65.9 us (25%)
  local copies, waits for them, and re-layouts  27.4 us (10%)
  matrix products  23.8 us (9%)
  between operations  16.4 us (6%)
  starting transfers between devices  15.1 us (6%)
    psum x2, waiting for transfers between devices, on_device(): gram_total = lax.psum(lax.psum(gram_local, 'grp'), 'slab')  104 us
    another operation x7, other arithmetic, on_device(): lower_factor = jnp.linalg.cholesky(gram_total)  34.6 us
    another operation x2, other arithmetic, on_device(): lax.linalg.triangular_solve(lower_factor, flat_rows.T, left_side=True, lo...  19.7 us
    dot_general x8, matrix products, on_device(): jnp.einsum('bij,bjr->bir', weights, other_rows, preferred_element_type=jn...  15.2 us
    gather x8, local copies, waits for them, and re-layouts, on_device(): other_rows = jnp.take(row_table, source_ids, axis=0)  12.8 us
    ppermute x4, starting transfers between devices, padded(): after = lax.ppermute(leading, axis, down)  9.91 us
    ppermute x4, waiting for transfers between devices, padded(): before = lax.ppermute(last, axis, up)  7.23 us
  transfers between devices with their start and end apart: 10, of which 5 were waited for; matrix products, arithmetic and copies ran while one was open for 6% of the time, Pallas kernels for 0%

profile of v1, /device:TPU:0, one launch (start us, length us, event | category | flops | bytes accessed | tf_op | source)
XLA Modules:
  0.0 260.8 jit_solution(10731194955963154727)
XLA Ops:
  7.2 0.7 convert_element_type.155
  8.0 3.0 %collective-permute-start = (bf16[1,4,3,128]{3,1,2,0:T(4,128)(2,1)S(1)}, bf16[1,4,3,128]{3,1,2,0:T(4,128)(2,1)S(1)}, u32[]{:S(2)}, u32[]{:S(2)}) collective-permute-start(bf16[1,4,3,128]{3,1,2,0:T(4,128)(2,1)S(1)} %get-tuple-element.121), channel_id=1, source_target_pairs={{0,4},{4,8},{8,12},{12,16},{16,20},{20,24},{24,28},{28,0},{1,5},{5... | collective-permute-start | bytes 9224 | tf_op jit(solution)/shard_map/ppermute | solution.py:15
  11.0 3.1 %collective-permute-start.1 = (bf16[1,4,3,128]{3,1,2,0:T(4,128)(2,1)S(1)}, bf16[1,4,3,128]{3,1,2,0:T(4,128)(2,1)S(1)}, u32[]{:S(2)}, u32[]{:S(2)}) collective-permute-start(bf16[1,4,3,128]{3,1,2,0:T(4,128)(2,1)S(1)} %get-tuple-element.122), channel_id=1, source_target_pairs={{4,0},{8,4},{12,8},{16,12},{20,16},{24,20},{28,24},{0,28},{5,1},{9... | collective-permute-start | bytes 9224 | tf_op jit(solution)/shard_map/ppermute | solution.py:16
  14.1 0.8 iota_compare_fusion.3
  14.9 1.5 broadcast_select_fusion
  16.5 4.7 %collective-permute-start.5 = (bf16[1,4,128,256]{3,2,1,0:T(8,128)(2,1)S(1)}, bf16[1,4,128,256]{3,2,1,0:T(8,128)(2,1)S(1)}, u32[]{:S(2)}, u32[]{:S(2)}) collective-permute-start(bf16[1,4,128,256]{3,2,1,0:T(8,128)(2,1)S(1)} %get-tuple-element.85), channel_id=1, source_target_pairs={{4,0},{8,4},{12,8},{16,12},{20,16},{24,20},{28,24},{0,28},{5,1},{9... | collective-permute-start | bytes 786440 | tf_op jit(solution)/shard_map/ppermute | solution.py:16
  21.3 0.7 fusion.121
  22.0 1.3 remainder_reduce_fusion
  26.2 1.7 collective-permute-start.3
  28.0 1.3 collective-permute-done.2
  34.4 0.7 slice_add_fusion.11
  36.6 1.7 collective-permute-start.6
  39.4 0.7 slice_add_fusion.15
  40.1 5.9 %collective-permute-done.6 = bf16[6,1,128,256]{3,2,1,0:T(8,128)(2,1)S(1)} collective-permute-done((bf16[6,1,128,256]{3,2,1,0:T(8,128)(2,1)S(1)}, bf16[6,1,128,256]{3,2,1,0:T(8,128)(2,1)S(1)}, u32[]{:S(2)}, u32[]{:S(2)}) %collective-permute-start.6) | collective-permute-done | bytes 393248 | tf_op jit(solution)/shard_map/ppermute | solution.py:15
  46.0 1.2 collective-permute-done.7
  47.2 1.4 pad_maximum_fusion
  49.2 1.7 gather_fusion.13
  50.9 1.7 gather_fusion.11
  52.6 1.7 gather_fusion.9
  54.3 1.7 gather_fusion.7
  56.0 1.7 gather_fusion.5
  57.8 1.8 gather_fusion.3
  59.6 1.8 gather_fusion.1
  61.4 2.4 fusion.5
  63.8 1.7 fusion.7
  65.6 1.7 fusion.9
  67.4 1.7 fusion.11
  69.2 1.7 fusion.13
  71.0 1.7 fusion.17
  72.7 1.7 fusion.15
  74.4 2.6 add_select_fusion
  77.0 4.2 %convolution_bitcast_fusion = f32[256,256]{0,1:T(8,128)} fusion(f32[16,128,256]{2,1,0:T(8,128)S(1)} %add_select_fusion), kind=kOutput, calls=%fused_computation.23 | convolution fusion | flops 1610612736 | bytes 2359296 | tf_op jit(solution)/shard_map/dot_general | solution.py:67
  81.5 29.6 %all-reduce.4.cloned.1.call-done = f32[256,256]{0,1:T(8,128)} async-done(((f32[256,256]{0,1:T(8,128)}), f32[256,256]{0,1:T(8,128)}) %all-reduce.4.cloned.1.call-update) | async-done | bytes 262160 | tf_op jit(solution)/shard_map/psum | solution.py:70
  111.1 74.2 %all-reduce.6.cloned.1.call-done = f32[256,256]{0,1:T(8,128)} async-done(((f32[256,256]{0,1:T(8,128)}), f32[256,256]{0,1:T(8,128)}) %all-reduce.6.cloned.1.call-update) | async-done | bytes 262160 | tf_op jit(solution)/shard_map/psum | solution.py:70
  185.4 1.1 copy.23
  186.4 1.0 fusion.107
  187.4 11.7 %cholesky.50 = f32[128,128]{1,0:T(8,128)S(1)} custom-call(f32[128,128]{1,0:T(8,128)S(1)} %cholesky.118), custom_call_target="Cholesky" | custom-call | tf_op jit(solution)/shard_map/jit(cholesky)/cholesky | solution.py:71
  199.8 9.8 %custom-call.14 = f32[1,128,128]{1,2,0:T(8,128)S(1)} custom-call(f32[1,128,128]{2,1,0:T(8,128)S(1)} %get-tuple-element.91), custom_call_target="InvertDiagBlocksLowerTriangular" | custom-call | tf_op jit(solution)/shard_map/jit(cholesky)/cholesky | solution.py:71
  210.1 11.7 %cholesky.105 = f32[128,128]{1,0:T(8,128)S(1)} custom-call(f32[128,128]{1,0:T(8,128)S(1)} %convolution_subtract_fusion.1), custom_call_target="Cholesky" | custom-call | tf_op jit(solution)/shard_map/jit(cholesky)/cholesky | solution.py:71
  223.9 0.8 copy.25
  224.8 4.0 %while.1 = (s32[]{:T(128)}, f32[256,256]{1,0:T(8,128)S(1)}, s32[2,2]{1,0:T(2,128)S(1)}, f32[2,128,128]{2,1,0:T(8,128)S(1)}, s32[]{:T(128)}) while((s32[]{:T(128)}, f32[256,256]{1,0:T(8,128)S(1)}, s32[2,2]{1,0:T(2,128)S(1)}, f32[2,128,128]{2,1,0:T(8,128)S(1)}, s32[]{:T(128)}) %tuple.117), condition=%wide.while_cond, body=%wide.while_body.sunk | while | flops 2 | bytes 131189 | solution.py:72
  225.5 1.3 bitcast_dynamic-update-slice_fusion.2
  227.5 1.3 bitcast_dynamic-update-slice_fusion.2
  228.9 19.7 %custom-call.15 = f32[2,128,128]{1,2,0:T(8,128)S(1)} custom-call(f32[2,128,128]{2,1,0:T(8,128)S(1)} %get-tuple-element.11), custom_call_target="InvertDiagBlocksLowerTriangular" | custom-call | tf_op jit(solution)/shard_map/triangular_solve | solution.py:72
  248.5 1.1 fusion.2
  249.6 1.8 convolution_subtract_fusion
  251.4 1.1 fusion.110
  252.7 1.3 copy.29
  (193 shorter events, 14.9 us)
Async XLA Ops:
  7.2 14.1 %copy-start.9 = (f32[4,4,3,128]{3,1,2,0:T(4,128)S(1)}, f32[4,4,3,128]{3,1,2,0:T(4,128)}, u32[]{:S(2)}) copy-start(f32[4,4,3,128]{3,1,2,0:T(4,128)} %param.8) | copy-start | bytes 73732
  7.2 14.0 %copy-start.20 = (s32[4,4]{1,0:T(4,128)S(1)}, s32[4,4]{1,0:T(4,128)}, u32[]{:S(2)}) copy-start(s32[4,4]{1,0:T(4,128)} %param.10) | copy-start | bytes 196
  7.2 14.1 %copy-start = (s32[4,4,8]{2,1,0:T(4,128)S(1)}, s32[4,4,8]{2,1,0:T(4,128)}, u32[]{:S(2)}) copy-start(s32[4,4,8]{2,1,0:T(4,128)} %param.11) | copy-start | bytes 1540
  7.2 103.9 %all-reduce.4.cloned.1.call-start = ((), (), s32[]{:S(2)}) async-start(), calls=%async_computation | async-start | bytes 524288 | tf_op jit(solution)/shard_map/psum | solution.py:70
  8.0 18.1 %collective-permute-start = (bf16[1,4,3,128]{3,1,2,0:T(4,128)(2,1)S(1)}, bf16[1,4,3,128]{3,1,2,0:T(4,128)(2,1)S(1)}, u32[]{:S(2)}, u32[]{:S(2)}) collective-permute-start(bf16[1,4,3,128]{3,1,2,0:T(4,128)(2,1)S(1)} %get-tuple-element.121), channel_id=1, source_target_pairs={{0,4},{4,8},{8,12},{12,16},{16,20},{20,24},{24,28},{28,0},{1,5},{5... | collective-permute-start | bytes 9224 | tf_op jit(solution)/shard_map/ppermute | solution.py:15
  11.0 15.1 %collective-permute-start.1 = (bf16[1,4,3,128]{3,1,2,0:T(4,128)(2,1)S(1)}, bf16[1,4,3,128]{3,1,2,0:T(4,128)(2,1)S(1)}, u32[]{:S(2)}, u32[]{:S(2)}) collective-permute-start(bf16[1,4,3,128]{3,1,2,0:T(4,128)(2,1)S(1)} %get-tuple-element.122), channel_id=1, source_target_pairs={{4,0},{8,4},{12,8},{16,12},{20,16},{24,20},{28,24},{0,28},{5,1},{9... | collective-permute-start | bytes 9224 | tf_op jit(solution)/shard_map/ppermute | solution.py:16
  16.4 20.0 %collective-permute-start.4 = (bf16[1,4,128,256]{3,2,1,0:T(8,128)(2,1)S(1)}, bf16[1,4,128,256]{3,2,1,0:T(8,128)(2,1)S(1)}, u32[]{:S(2)}, u32[]{:S(2)}) collective-permute-start(bf16[1,4,128,256]{3,2,1,0:T(8,128)(2,1)S(1)} %get-tuple-element.84), channel_id=1, source_target_pairs={{0,4},{4,8},{8,12},{12,16},{16,20},{20,24},{24,28},{28,0},{1,5},{5... | collective-permute-start | bytes 786440 | tf_op jit(solution)/shard_map/ppermute | solution.py:15
  16.5 20.0 %collective-permute-start.5 = (bf16[1,4,128,256]{3,2,1,0:T(8,128)(2,1)S(1)}, bf16[1,4,128,256]{3,2,1,0:T(8,128)(2,1)S(1)}, u32[]{:S(2)}, u32[]{:S(2)}) collective-permute-start(bf16[1,4,128,256]{3,2,1,0:T(8,128)(2,1)S(1)} %get-tuple-element.85), channel_id=1, source_target_pairs={{4,0},{8,4},{12,8},{16,12},{20,16},{24,20},{28,24},{0,28},{5,1},{9... | collective-permute-start | bytes 786440 | tf_op jit(solution)/shard_map/ppermute | solution.py:16
  25.8 7.3 %copy-start.28 = (pred[16]{0:T(512)(128)(4,1)}, pred[16]{0:T(512)(128)(4,1)S(1)}, u32[]{:S(2)}) copy-start(pred[16]{0:T(512)(128)(4,1)S(1)} %get-tuple-element.50) | copy-start | bytes 52
  25.9 7.3 %copy-start.42 = (pred[16]{0:T(512)(128)(4,1)}, pred[16]{0:T(512)(128)(4,1)S(1)}, u32[]{:S(2)}) copy-start(pred[16]{0:T(512)(128)(4,1)S(1)} %get-tuple-element.123) | copy-start | bytes 52
  25.9 7.9 %copy-start.34 = (pred[16]{0:T(512)(128)(4,1)}, pred[16]{0:T(512)(128)(4,1)S(1)}, u32[]{:S(2)}) copy-start(pred[16]{0:T(512)(128)(4,1)S(1)} %get-tuple-element.131) | copy-start | bytes 52
  25.9 7.9 %copy-start.36 = (pred[16]{0:T(512)(128)(4,1)}, pred[16]{0:T(512)(128)(4,1)S(1)}, u32[]{:S(2)}) copy-start(pred[16]{0:T(512)(128)(4,1)S(1)} %get-tuple-element.129) | copy-start | bytes 52
  25.9 7.9 %copy-start.38 = (pred[16]{0:T(512)(128)(4,1)}, pred[16]{0:T(512)(128)(4,1)S(1)}, u32[]{:S(2)}) copy-start(pred[16]{0:T(512)(128)(4,1)S(1)} %get-tuple-element.127) | copy-start | bytes 52
  25.9 7.9 %copy-start.40 = (pred[16]{0:T(512)(128)(4,1)}, pred[16]{0:T(512)(128)(4,1)S(1)}, u32[]{:S(2)}) copy-start(pred[16]{0:T(512)(128)(4,1)S(1)} %get-tuple-element.125) | copy-start | bytes 52
  25.9 13.5 %copy-start.30 = (pred[16]{0:T(512)(128)(4,1)}, pred[16]{0:T(512)(128)(4,1)S(1)}, u32[]{:S(2)}) copy-start(pred[16]{0:T(512)(128)(4,1)S(1)} %get-tuple-element.133) | copy-start | bytes 52
  25.9 13.5 %copy-start.32 = (pred[16]{0:T(512)(128)(4,1)}, pred[16]{0:T(512)(128)(4,1)S(1)}, u32[]{:S(2)}) copy-start(pred[16]{0:T(512)(128)(4,1)S(1)} %get-tuple-element.135) | copy-start | bytes 52
  25.9 7.2 %copy-start.21 = (s32[1024]{0:T(1024)}, s32[1024]{0:T(1024)S(1)}, u32[]{:S(2)}) copy-start(s32[1024]{0:T(1024)S(1)} %pad_clamp_fusion.1) | copy-start | bytes 12292
  26.0 4.6 %copy-start.22 = (s32[1024]{0:T(1024)}, s32[1024]{0:T(1024)S(1)}, u32[]{:S(2)}) copy-start(s32[1024]{0:T(1024)S(1)} %pad_clamp_fusion.2) | copy-start | bytes 12292
  26.0 5.2 %copy-start.23 = (s32[1024]{0:T(1024)}, s32[1024]{0:T(1024)S(1)}, u32[]{:S(2)}) copy-start(s32[1024]{0:T(1024)S(1)} %pad_clamp_fusion.3) | copy-start | bytes 12292
  26.0 5.7 %copy-start.24 = (s32[1024]{0:T(1024)}, s32[1024]{0:T(1024)S(1)}, u32[]{:S(2)}) copy-start(s32[1024]{0:T(1024)S(1)} %pad_clamp_fusion.4) | copy-start | bytes 12292
  26.0 7.1 %copy-start.25 = (s32[1024]{0:T(1024)}, s32[1024]{0:T(1024)S(1)}, u32[]{:S(2)}) copy-start(s32[1024]{0:T(1024)S(1)} %pad_clamp_fusion.5) | copy-start | bytes 12292
  26.1 14.0 %copy-start.26 = (s32[1024]{0:T(1024)}, s32[1024]{0:T(1024)S(1)}, u32[]{:S(2)}) copy-start(s32[1024]{0:T(1024)S(1)} %pad_clamp_fusion.6) | copy-start | bytes 12292
  26.2 3.1 %collective-permute-start.2 = (bf16[6,1,3,128]{3,1,2,0:T(2,128)(2,1)S(1)}, bf16[6,1,3,128]{3,1,2,0:T(2,128)(2,1)S(1)}, u32[]{:S(2)}, u32[]{:S(2)}) collective-permute-start(bf16[6,1,3,128]{3,1,2,0:T(2,128)(2,1)S(1)} %get-tuple-element.119), channel_id=1, source_target_pairs={{0,1},{1,2},{2,3},{3,0},{4,5},{5,6},{6,7},{7,4},{8,9},{9,10},{10,1... | collective-permute-start | bytes 13832 | tf_op jit(solution)/shard_map/ppermute | solution.py:15
  26.2 3.1 %collective-permute-start.3 = (bf16[6,1,3,128]{3,1,2,0:T(2,128)(2,1)S(1)}, bf16[6,1,3,128]{3,1,2,0:T(2,128)(2,1)S(1)}, u32[]{:S(2)}, u32[]{:S(2)}) collective-permute-start(bf16[6,1,3,128]{3,1,2,0:T(2,128)(2,1)S(1)} %get-tuple-element.120), channel_id=1, source_target_pairs={{1,0},{2,1},{3,2},{0,3},{5,4},{6,5},{7,6},{4,7},{9,8},{10,9},{11,1... | collective-permute-start | bytes 13832 | tf_op jit(solution)/shard_map/ppermute | solution.py:16
  28.0 18.0 %copy-start.27 = (s32[1024]{0:T(1024)}, s32[1024]{0:T(1024)S(1)}, u32[]{:S(2)}) copy-start(s32[1024]{0:T(1024)S(1)} %pad_clamp_fusion.7) | copy-start | bytes 12292
  36.4 9.6 %copy-start.1 = (bf16[1,4,128,256]{3,2,1,0:T(8,128)(2,1)}, bf16[1,4,128,256]{3,2,1,0:T(8,128)(2,1)S(1)}, u32[]{:S(2)}) copy-start(bf16[1,4,128,256]{3,2,1,0:T(8,128)(2,1)S(1)} %collective-permute-done.4) | copy-start | bytes 786436
  36.5 9.5 %copy-start.2 = (bf16[1,4,128,256]{3,2,1,0:T(8,128)(2,1)}, bf16[1,4,128,256]{3,2,1,0:T(8,128)(2,1)S(1)}, u32[]{:S(2)}) copy-start(bf16[1,4,128,256]{3,2,1,0:T(8,128)(2,1)S(1)} %collective-permute-done.5) | copy-start | bytes 786436
  36.6 9.4 %collective-permute-start.6 = (bf16[6,1,128,256]{3,2,1,0:T(8,128)(2,1)S(1)}, bf16[6,1,128,256]{3,2,1,0:T(8,128)(2,1)S(1)}, u32[]{:S(2)}, u32[]{:S(2)}) collective-permute-start(bf16[6,1,128,256]{3,2,1,0:T(8,128)(2,1)S(1)} %get-tuple-element.82), channel_id=1, source_target_pairs={{0,1},{1,2},{2,3},{3,0},{4,5},{5,6},{6,7},{7,4},{8,9},{9,10},{10,1... | collective-permute-start | bytes 1179656 | tf_op jit(solution)/shard_map/ppermute | solution.py:15
  38.3 8.9 %collective-permute-start.7 = (bf16[6,1,128,256]{3,2,1,0:T(8,128)(2,1)S(1)}, bf16[6,1,128,256]{3,2,1,0:T(8,128)(2,1)S(1)}, u32[]{:S(2)}, u32[]{:S(2)}) collective-permute-start(bf16[6,1,128,256]{3,2,1,0:T(8,128)(2,1)S(1)} %get-tuple-element.83), channel_id=1, source_target_pairs={{1,0},{2,1},{3,2},{0,3},{5,4},{6,5},{7,6},{4,7},{9,8},{10,9},{11,1... | collective-permute-start | bytes 1179656 | tf_op jit(solution)/shard_map/ppermute | solution.py:16
  57.8 3.6 %copy-start.43 = (pred[16]{0:T(512)(128)(4,1)S(1)}, pred[16]{0:T(512)(128)(4,1)}, u32[]{:S(2)}) copy-start(pred[16]{0:T(512)(128)(4,1)} %copy-done.42) | copy-start | bytes 52
  61.4 2.4 copy-start.8
  61.4 2.4 copy-start.41
  67.3 1.8 copy-start.5
  67.3 1.8 copy-start.11
  67.3 1.8 copy-start.12
  67.3 1.8 copy-start.13
  67.4 1.8 copy-start.35
  69.1 1.8 copy-start.4
  69.1 1.8 copy-start.17
  69.1 1.8 copy-start.18
  69.1 1.8 copy-start.19
  69.2 1.8 copy-start.33
  70.9 1.8 copy-start.3
  70.9 1.8 copy-start.14
  70.9 1.8 copy-start.15
  70.9 1.8 copy-start.16
  71.0 1.8 copy-start.31
  81.2 104.1 %all-reduce.6.cloned.1.call-start = ((), (), s32[]{:S(2)}) async-start(), calls=%async_computation.1 | async-start | bytes 524288 | tf_op jit(solution)/shard_map/psum | solution.py:70
  (6 other events, 10.4 us)
Sparse Core Ops, SparseCore 0:
  81.3 29.6 all-reduce.3
  114.8 70.5 all-reduce.5
